TPU v7x, 256 devices: a whole 4x4x8 slice. The times are simulated.
256 devices in a mesh: dp: 16 (over x, y_hi, core), seq: 16 (over z, y_lo).
Axes of the slice: x: 4, y: 4 (y_hi: 2, y_lo: 2; y = y_hi * 2 + y_lo), z: 8, core: 2. Of those that a mesh axis runs over, the one named last changes fastest.
Arguments:
- coarse: bfloat16 [16, 4096, 1024], P('dp', 'seq'), may hold values from -6 to 6
- skip: bfloat16 [16, 8192, 768], P('dp', 'seq'), may hold values from -6 to 6
- conv_weight: bfloat16 [5, 1024, 768], replicated, may hold values from -0.078125 to 0.078125
- donor_weight: bfloat16 [768, 768], replicated, may hold values from -0.21875 to 0.21875
- acceptor_weight: bfloat16 [768, 768], replicated, may hold values from -0.21875 to 0.21875
- other_grad: bfloat16 [16, 8192, 768], P('dp', 'seq'), may hold values from -4 to 4
- score_grad: float32 [16, 1024], P('dp', 'seq'), may hold values from -16 to 16
- donor_pos: int32 [16, 1024], P('dp', 'seq'), may hold values from 0 to 511
- acceptor_pos: int32 [16, 1024], P('dp', 'seq'), may hold values from 0 to 8191, as said below
- pair_mask: int32 [16, 1024], P('dp', 'seq'), may hold values 0 or 1
Outputs:
- scores: float32 [16, 1024], P('dp', 'seq')
- coarse_grad: bfloat16 [16, 4096, 1024], P('dp', 'seq')
- donor_weight_grad: float32 [768, 768], P('seq')
- acceptor_weight_grad: float32 [768, 768], P('seq')
Inputs may be any that keep to these rules, and one draw needn't show every extreme that they name: Position in the whole sample. Among the 64 slots held by one shard of a sample, at most 8 have their acceptor on any one shard (shard = acceptor_pos // 512); in every sample some shard is named by exactly 8 slots of every shard.
All inputs are finite; a program needn't handle non-finite values. No bound on the sum of `pair_mask` on one device may be relied on, other than what follows from the above.
Results may differ from a plain program's by a relative error of at most 0.013.
Values may be sent and summed in bfloat16 or wider, within the bound.
A program may use at most 128 MiB of HBM per device.

v0:
```python
import math
import jax
import jax.numpy as jnp
from jax import lax
from jax.sharding import PartitionSpec as P

ACAP = 8


def with_halo(cells, sides, width):
    for axis, dim in sides:
        count = lax.axis_size(axis)
        ends = count - 1
        head = lax.slice_in_dim(cells, 0, width, axis=dim)
        tail = lax.slice_in_dim(cells, cells.shape[dim] - width, cells.shape[dim], axis=dim)
        cells = jnp.concatenate(
            [
                lax.ppermute(tail, axis, [(i, (i + 1) % count) for i in range(ends)]),
                cells,
                lax.ppermute(head, axis, [((i + 1) % count, i) for i in range(ends)]),
            ],
            axis=dim,
        )
    return cells


def activate(values):
    return jax.nn.gelu(values, approximate=True)


def on_device(
    coarse,
    skip,
    conv_weight,
    donor_weight,
    acceptor_weight,
    other_grad,
    score_grad,
    donor_pos,
    acceptor_pos,
    pair_mask,
):
    seq_count = lax.axis_size("seq")
    batch_count = lax.axis_size("dp")
    taps = conv_weight.shape[0]
    emb_width = donor_weight.shape[1]
    inverse_root = 1.0 / math.sqrt(emb_width)
    widened = with_halo(coarse, (("seq", 1),), 1)
    upsampled = jnp.repeat(widened[0], 2, axis=0)
    row_count = upsampled.shape[0] - 4
    preact = skip[0].astype(jnp.float32)
    for shift_index in range(taps):
        preact = preact + jnp.dot(
            upsampled[shift_index : shift_index + row_count],
            conv_weight[shift_index],
            preferred_element_type=jnp.float32,
        )
    activated = activate(preact).astype(jnp.bfloat16)
    donor_rows = donor_pos[0]
    donor_act = activated[donor_rows]
    donor_emb = jnp.dot(donor_act, donor_weight, preferred_element_type=jnp.float32).astype(
        jnp.bfloat16
    )
    targets = acceptor_pos[0]
    owner = targets // row_count
    local_row = targets % row_count
    owner_hits = (owner[:, None] == jnp.arange(seq_count, dtype=jnp.int32)[None, :]).astype(
        jnp.int32
    )
    place_rank = jnp.sum((jnp.cumsum(owner_hits, axis=0) - owner_hits) * owner_hits, axis=1)
    capacity = ACAP
    slot_index = owner * capacity + place_rank
    requests = (
        jnp.zeros((seq_count * capacity,), jnp.int32)
        .at[slot_index]
        .set(local_row)
        .reshape(seq_count, capacity)
    )
    received = lax.all_to_all(requests, "seq", split_axis=0, concat_axis=0, tiled=True)
    wanted = activated[received.reshape(-1)]
    projected = jnp.dot(wanted, acceptor_weight, preferred_element_type=jnp.float32).astype(
        jnp.bfloat16
    )
    projected = projected.reshape(received.shape[0], received.shape[1], emb_width)
    returned = lax.all_to_all(projected, "seq", split_axis=0, concat_axis=0, tiled=True)
    returned, served_rows = (returned, received)
    acceptor_emb = returned.reshape(seq_count * capacity, emb_width)[slot_index]
    mask_float = pair_mask[0].astype(jnp.float32)
    scores = (
        mask_float
        * jnp.sum(donor_emb.astype(jnp.float32) * acceptor_emb.astype(jnp.float32), axis=1)
        * inverse_root
    )
    weighted = score_grad[0] * mask_float
    donor_emb_grad = (weighted[:, None] * acceptor_emb.astype(jnp.float32) * inverse_root).astype(
        jnp.bfloat16
    )
    acceptor_emb_grad = (weighted[:, None] * donor_emb.astype(jnp.float32) * inverse_root).astype(
        jnp.bfloat16
    )
    outgoing = (
        jnp.zeros((seq_count * capacity, emb_width), jnp.bfloat16)
        .at[slot_index]
        .set(acceptor_emb_grad)
    )
    outgoing = outgoing.reshape(seq_count, capacity, emb_width)
    received = lax.all_to_all(outgoing, "seq", split_axis=0, concat_axis=0, tiled=True)
    flattened = received.reshape(-1, emb_width)
    to_rows = jnp.dot(flattened, acceptor_weight.T, preferred_element_type=jnp.float32)
    row_terms = to_rows.reshape(received.shape[0], received.shape[1], -1)
    served_flat = served_rows.reshape(-1)
    act_grad = other_grad[0].astype(jnp.float32)
    act_grad = act_grad.at[donor_rows].add(
        jnp.dot(donor_emb_grad, donor_weight.T, preferred_element_type=jnp.float32)
    )
    act_grad = act_grad.at[served_flat].add(row_terms.reshape(-1, row_terms.shape[2]))
    pull = jax.vjp(activate, preact)[1]
    preact_grad = pull(act_grad)[0].astype(jnp.bfloat16)
    widened_grad = with_halo(preact_grad[None], (("seq", 1),), 2)[0]
    upsampled_grad = jnp.zeros((row_count, conv_weight.shape[1]), jnp.float32)
    for shift_index in range(taps):
        begin = 4 - shift_index
        upsampled_grad = upsampled_grad + jnp.dot(
            widened_grad[begin : begin + row_count],
            conv_weight[shift_index].T,
            preferred_element_type=jnp.float32,
        )
    coarse_grad = (
        upsampled_grad.reshape(row_count // 2, 2, -1).sum(axis=1).astype(jnp.bfloat16)[None]
    )
    served_act = activated[served_flat]
    served_emb_grad = received.reshape(-1, emb_width)
    rows_each = donor_weight.shape[0] // seq_count
    factor = 1.0 / batch_count
    donor_term = jnp.dot(donor_act.T, donor_emb_grad, preferred_element_type=jnp.float32)
    acceptor_term = jnp.dot(served_act.T, served_emb_grad, preferred_element_type=jnp.float32)
    donor_total, acceptor_total = lax.psum((donor_term, acceptor_term), ("dp", "seq"))
    first_row = lax.axis_index("seq") * rows_each
    donor_part = lax.dynamic_slice_in_dim(donor_total, first_row, rows_each, 0)
    acceptor_part = lax.dynamic_slice_in_dim(acceptor_total, first_row, rows_each, 0)
    return (scores[None], coarse_grad, donor_part * factor, acceptor_part * factor)


def solution(mesh):
    in_specs = (
        P("dp", "seq", None),
        P("dp", "seq", None),
        P(),
        P(),
        P(),
        P("dp", "seq", None),
        P("dp", "seq"),
        P("dp", "seq"),
        P("dp", "seq"),
        P("dp", "seq"),
    )
    out_specs = (P("dp", "seq"), P("dp", "seq", None), P("seq", None), P("seq", None))
    return jax.shard_map(
        on_device, mesh=mesh, in_specs=in_specs, out_specs=out_specs, check_vma=False
    )
```

profile of v0, /device:TPU:2, one launch (start us, length us, event | category | flops | bytes accessed | tf_op | source)
XLA Modules:
  0.0 379.7 jit_solution(3904731837600903716)
XLA Ops:
  7.2 0.0 copy-start
  7.2 0.8 fusion.89
  8.0 3.5 collective-permute-start
  11.5 1.3 collective-permute-start.1
  12.8 0.7 and_select_fusion
  13.5 0.1 fusion.71
  13.6 0.1 reduce_window_sum.11
  13.7 0.2 select_reduce_fusion
  13.8 0.7 fusion.77
  14.5 0.8 scatter_custom_fusion
  15.3 0.7 all_to_all.12
  16.0 11.7 %all-to-all-start = ((s32[16,1,8]{2,1,0:T(1,128)}), s32[16,1,8]{2,1,0:T(1,128)S(1)}, u32[]{:S(2)}, u32[]{:S(2)}) async-start(s32[16,1,8]{2,1,0:T(1,128)} %bitcast.16), calls=%async_computation | async-start | bytes 16384 | tf_op jit(solution)/shard_map/all_to_all | solution.py:79
  27.8 1.6 broadcast_in_dim.14
  29.3 0.4 slice.107
  29.8 3.6 fusion.20
  33.4 2.7 all-to-all-done
  36.2 0.5 broadcast.232
  36.7 0.7 reduce.3
  37.4 0.1 reshape.228
  37.5 0.1 maximum_bitcast_fusion
  37.6 0.5 broadcast_in_dim.13
  38.2 1.4 reshape.227
  39.6 4.0 %fusion.16 = f32[512,768]{1,0:T(8,128)} fusion(bf16[5,1024,768]{2,1,0:T(8,128)(2,1)} %param.12, bf16[516,1024]{1,0:T(8,128)(2,1)} %reshape.227), kind=kOutput, calls=%fused_computation.27 | convolution fusion | flops 805306368 | bytes 4194304 | tf_op jit(solution)/shard_map/dot_general | solution.py:53
  43.6 3.6 fusion.24
  47.1 1.0 fusion.59
  48.1 0.5 broadcast_in_dim.15
  48.7 0.4 slice.113
  49.1 3.6 fusion.12
  52.7 0.5 broadcast_in_dim.12
  53.3 0.4 slice.101
  53.7 6.1 %multiply_convert_fusion = (bf16[512,768]{1,0:T(8,128)(2,1)S(1)}, f32[512,768]{1,0:T(8,128)}) fusion(f32[512,768]{1,0:T(8,128)} %fusion.12, f32[512,768]{1,0:T(8,128)} %fusion.16, f32[512,768]{1,0:T(8,128)} %fusion.20, f32[512,768]{1,0:T(8,128)} %fusion.24, bf16[512,1024]{1,0:T(8,128)(2,1)S(1)} %slice.101, bf16[5,1024,768]{2,1,0:T(8,128)(2,1)} %param.12, ...), kind=kOutput, calls=%fused_computation.41 | convolution fusion | flops 811204608 | bytes 12058624 | tf_op jit(solution)/shard_map/dot_general | solution.py:53
  59.8 0.9 gather_fusion.1
  60.7 1.0 fusion.40
  61.7 5.4 %all-to-all-start.1 = ((bf16[16,8,768]{2,1,0:T(8,128)(2,1)}), bf16[16,8,768]{2,1,0:T(8,128)(2,1)}, u32[]{:S(2)}, u32[]{:S(2)}) async-start(bf16[16,8,768]{2,1,0:T(8,128)(2,1)} %fusion.40), calls=%async_computation.1 | async-start | bytes 393216 | tf_op jit(solution)/shard_map/all_to_all | solution.py:85
  67.2 1.2 bitcast_convert_fusion
  68.4 1.3 gather_fusion
  69.8 7.8 %all-to-all-done.1 = bf16[16,8,768]{2,1,0:T(8,128)(2,1)} async-done(((bf16[16,8,768]{2,1,0:T(8,128)(2,1)}), bf16[16,8,768]{2,1,0:T(8,128)(2,1)}, u32[]{:S(2)}, u32[]{:S(2)}) %all-to-all-start.1) | async-done | bytes 196640 | tf_op jit(solution)/shard_map/all_to_all | solution.py:85
  77.5 1.7 gather_fusion.2
  79.3 1.8 fusion.60
  81.1 0.5 multiply_bitcast_fusion
  81.6 1.7 scatter_custom_fusion.2
  83.3 3.5 all-to-all-start.2
  86.8 0.2 all-reduce.3.cloned.1.call-start
  87.0 1.8 fusion.74
  88.8 0.0 copy-start.6
  88.8 1.6 scatter_fusion
  90.4 1.9 fusion.72
  92.4 4.5 %all-to-all-done.2 = bf16[16,8,768]{2,1,0:T(8,128)(2,1)S(1)} async-done(((bf16[16,8,768]{2,1,0:T(8,128)(2,1)}), bf16[16,8,768]{2,1,0:T(8,128)(2,1)S(1)}, u32[]{:S(2)}, u32[]{:S(2)}) %all-to-all-start.2) | async-done | bytes 196640 | tf_op jit(solution)/shard_map/all_to_all | solution.py:107
  96.9 1.3 fusion.65
  98.2 2.5 scatter_fusion.1
  100.6 2.0 fusion.63
  102.6 0.0 all-reduce.3.cloned.1.call-update
  102.7 2.6 fusion.6
  105.3 1.6 collective-permute-start.2
  106.9 2.4 fusion.18
  109.3 4.5 %collective-permute-start.3 = (bf16[1,2,768]{2,1,0:T(2,128)(2,1)S(1)}, bf16[1,2,768]{2,1,0:T(2,128)(2,1)S(1)}, u32[]{:S(2)}, u32[]{:S(2)}) collective-permute-start(bf16[1,2,768]{2,1,0:T(2,128)(2,1)S(1)} %get-tuple-element.7), channel_id=1, source_target_pairs={{0,1},{1,2},{2,3},{3,4},{4,5},{5,6},{6,7},{7,8},{8,9},{9,10},{10,1... | collective-permute-start | bytes 9224 | tf_op jit(solution)/shard_map/ppermute | solution.py:18
  113.9 2.4 fusion.26
  116.3 1.0 fusion.22
  117.3 1.0 fusion.14
  118.4 2.4 add_add_fusion
  120.8 2.5 reshape.233
  123.3 3.6 reduce_sum.35
  126.9 244.2 %all-reduce.3.cloned.1.call-done = (f32[768,768]{1,0:T(8,128)}, f32[768,768]{1,0:T(8,128)}) async-done(((f32[768,768]{1,0:T(8,128)}, f32[768,768]{1,0:T(8,128)}), (f32[768,768]{1,0:T(8,128)}, f32[768,768]{1,0:T(8,128)})) %all-reduce.3.cloned.1.call-update) | async-done | bytes 4718608 | tf_op jit(solution)/shard_map/psum | solution.py:137
  371.1 1.7 dynamic-slice_multiply_fusion
  (35 shorter events, 0.1 us)
Async XLA Ops:
  7.2 53.5 %copy-start = (bf16[768,768]{1,0:T(8,128)(2,1)S(1)}, bf16[768,768]{1,0:T(8,128)(2,1)}, u32[]{:S(2)}) copy-start(bf16[768,768]{1,0:T(8,128)(2,1)} %param.14) | copy-start | bytes 3538948
  8.0 29.4 %collective-permute-start = (bf16[1,1,1024]{2,1,0:T(2,128)(2,1)S(1)}, bf16[1,1,1024]{2,1,0:T(2,128)(2,1)S(1)}, u32[]{:S(2)}, u32[]{:S(2)}) collective-permute-start(bf16[1,1,1024]{2,1,0:T(2,128)(2,1)S(1)} %get-tuple-element.10), channel_id=1, source_target_pairs={{0,1},{1,2},{2,3},{3,4},{4,5},{5,6},{6,7},{7,8},{8,9},{9,10},{10,1... | collective-permute-start | bytes 6152 | tf_op jit(solution)/shard_map/ppermute | solution.py:18
  11.5 26.0 %collective-permute-start.1 = (bf16[1,1,1024]{2,1,0:T(2,128)(2,1)S(1)}, bf16[1,1,1024]{2,1,0:T(2,128)(2,1)S(1)}, u32[]{:S(2)}, u32[]{:S(2)}) collective-permute-start(bf16[1,1,1024]{2,1,0:T(2,128)(2,1)S(1)} %get-tuple-element.11), channel_id=1, source_target_pairs={{1,0},{2,1},{3,2},{4,3},{5,4},{6,5},{7,6},{8,7},{9,8},{10,9},{11,1... | collective-permute-start | bytes 6152 | tf_op jit(solution)/shard_map/ppermute | solution.py:20
  14.5 18.9 %copy-start.9 = (s32[64]{0:T(128)}, s32[64]{0:T(128)S(1)}, u32[]{:S(2)}) copy-start(s32[64]{0:T(128)S(1)} %fusion.77) | copy-start | bytes 772
  16.0 20.2 %all-to-all-start = ((s32[16,1,8]{2,1,0:T(1,128)}), s32[16,1,8]{2,1,0:T(1,128)S(1)}, u32[]{:S(2)}, u32[]{:S(2)}) async-start(s32[16,1,8]{2,1,0:T(1,128)} %bitcast.16), calls=%async_computation | async-start | bytes 16384 | tf_op jit(solution)/shard_map/all_to_all | solution.py:79
  27.7 2.1 copy-start.10
  29.8 7.7 %copy-start.1 = (bf16[1,256,1024]{2,1,0:T(8,128)(2,1)S(1)}, bf16[1,256,1024]{2,1,0:T(8,128)(2,1)}, u32[]{:S(2)}) copy-start(bf16[1,256,1024]{2,1,0:T(8,128)(2,1)} %param.10) | copy-start | bytes 1572868
  39.6 4.0 %copy-start.5 = (bf16[516,1024]{1,0:T(8,128)(2,1)S(1)}, bf16[516,1024]{1,0:T(8,128)(2,1)}, u32[]{:S(2)}) copy-start(bf16[516,1024]{1,0:T(8,128)(2,1)} %reshape.227) | copy-start | bytes 3170308
  49.1 3.6 copy-start.2
  60.7 6.5 %copy-start.3 = (bf16[128,768]{1,0:T(8,128)(2,1)}, bf16[128,768]{1,0:T(8,128)(2,1)S(1)}, u32[]{:S(2)}) copy-start(bf16[128,768]{1,0:T(8,128)(2,1)S(1)} %gather_fusion.1) | copy-start | bytes 589828
  61.7 15.8 %all-to-all-start.1 = ((bf16[16,8,768]{2,1,0:T(8,128)(2,1)}), bf16[16,8,768]{2,1,0:T(8,128)(2,1)}, u32[]{:S(2)}, u32[]{:S(2)}) async-start(bf16[16,8,768]{2,1,0:T(8,128)(2,1)} %fusion.40), calls=%async_computation.1 | async-start | bytes 393216 | tf_op jit(solution)/shard_map/all_to_all | solution.py:85
  69.8 11.3 %copy-start.7 = (f32[1,64]{1,0:T(1,128)S(1)}, f32[1,64]{1,0:T(1,128)}, u32[]{:S(2)}) copy-start(f32[1,64]{1,0:T(1,128)} %param.16) | copy-start | bytes 772
  69.8 11.3 %copy-start.8 = (s32[1,64]{1,0:T(1,128)S(1)}, s32[1,64]{1,0:T(1,128)}, u32[]{:S(2)}) copy-start(s32[1,64]{1,0:T(1,128)} %param.19) | copy-start | bytes 772
  83.3 13.6 %all-to-all-start.2 = ((bf16[16,8,768]{2,1,0:T(8,128)(2,1)}), bf16[16,8,768]{2,1,0:T(8,128)(2,1)S(1)}, u32[]{:S(2)}, u32[]{:S(2)}) async-start(bf16[16,8,768]{2,1,0:T(8,128)(2,1)} %bitcast.23), calls=%async_computation.2 | async-start | bytes 393216 | tf_op jit(solution)/shard_map/all_to_all | solution.py:107
  86.8 284.3 %all-reduce.3.cloned.1.call-start = ((), (), s32[]{:S(2)}) async-start(), calls=%async_computation.3 | async-start | bytes 9437184 | tf_op jit(solution)/shard_map/psum | solution.py:137
  88.8 1.6 copy-start.6
  98.2 2.5 copy-start.4
  102.7 13.6 %slice-start = ((s8[7864320]{0:T(1024)(128)(4,1)}), s8[4194304]{0:T(1024)(128)(4,1)S(1)}, s32[]{:S(2)}) async-start(s8[7864320]{0:T(1024)(128)(4,1)} %bitcast.129), calls=%async_computation.4 | async-start | bytes 8388608
  105.3 11.0 %slice-start.1 = ((s8[7864320]{0:T(1024)(128)(4,1)}), s8[3670016]{0:T(1024)(128)(4,1)S(1)}, s32[]{:S(2)}) async-start(s8[7864320]{0:T(1024)(128)(4,1)} %bitcast.129), calls=%async_computation.5 | async-start | bytes 7340032
  105.3 8.5 %collective-permute-start.2 = (bf16[1,2,768]{2,1,0:T(2,128)(2,1)S(1)}, bf16[1,2,768]{2,1,0:T(2,128)(2,1)S(1)}, u32[]{:S(2)}, u32[]{:S(2)}) collective-permute-start(bf16[1,2,768]{2,1,0:T(2,128)(2,1)S(1)} %get-tuple-element.6), channel_id=1, source_target_pairs={{1,0},{2,1},{3,2},{4,3},{5,4},{6,5},{7,6},{8,7},{9,8},{10,9},{11,1... | collective-permute-start | bytes 9224 | tf_op jit(solution)/shard_map/ppermute | solution.py:20
  109.3 8.0 %collective-permute-start.3 = (bf16[1,2,768]{2,1,0:T(2,128)(2,1)S(1)}, bf16[1,2,768]{2,1,0:T(2,128)(2,1)S(1)}, u32[]{:S(2)}, u32[]{:S(2)}) collective-permute-start(bf16[1,2,768]{2,1,0:T(2,128)(2,1)S(1)} %get-tuple-element.7), channel_id=1, source_target_pairs={{0,1},{1,2},{2,3},{3,4},{4,5},{5,6},{6,7},{7,8},{8,9},{9,10},{10,1... | collective-permute-start | bytes 9224 | tf_op jit(solution)/shard_map/ppermute | solution.py:18
Sparse Core Ops, SparseCore 0:
  102.8 268.2 all-reduce.2
where the time goes:
time: 380 us
  waiting for transfers between devices  259 us (68%)
  matrix products  39.8 us (10%)
  starting transfers between devices  31.8 us (8%)
  other arithmetic  18.9 us (5%)
  local copies, waits for them, and re-layouts  15.4 us (4%)
  between operations  14.5 us (4%)
    psum x1, waiting for transfers between devices, on_device(): lax.psum((donor_term, acceptor_term), ('dp', 'seq'))  244 us
    dot_general x5, matrix products, on_device(): jnp.dot(upsampled[shift_index:shift_index + row_count], conv_weight[shift...  20.8 us
    all_to_all x1, starting transfers between devices, on_device(): lax.all_to_all(requests, 'seq', split_axis=0, concat_axis=0, tiled=True)  11.7 us
    dot_general x5, matrix products, on_device(): jnp.dot(widened_grad[begin:begin + row_count], conv_weight[shift_index].T...  9.29 us
    ppermute x2, starting transfers between devices, with_halo(): lax.ppermute(tail, axis, [(i, (i + 1) % count) for i in range(ends)])  8.02 us
    all_to_all x1, waiting for transfers between devices, on_device(): lax.all_to_all(projected, 'seq', split_axis=0, concat_axis=0, tiled=True)  7.75 us
  transfers between devices with their start and end apart: 8, of which 4 were waited for; matrix products, arithmetic and copies ran while one was open for 9% of the time, Pallas kernels for 0%

commit v1 on v0

--- a/solution.py
+++ b/solution.py
@@ -134,7 +134,7 @@
     factor = 1.0 / batch_count
     donor_term = jnp.dot(donor_act.T, donor_emb_grad, preferred_element_type=jnp.float32)
     acceptor_term = jnp.dot(served_act.T, served_emb_grad, preferred_element_type=jnp.float32)
-    donor_total, acceptor_total = lax.psum((donor_term, acceptor_term), ("dp", "seq"))
+    donor_total, acceptor_total = lax.psum(lax.psum((donor_term, acceptor_term), "dp"), "seq")
     first_row = lax.axis_index("seq") * rows_each
     donor_part = lax.dynamic_slice_in_dim(donor_total, first_row, rows_each, 0)
     acceptor_part = lax.dynamic_slice_in_dim(acceptor_total, first_row, rows_each, 0)

time: 380 us -> 488 us (1.28)
  waiting for transfers between devices: 259 us -> 368 us
    psum x1 -> x2, waiting for transfers between devices: 244 us -> 349 us  [the longest x1 198 us: on_device(): lax.psum(lax.psum((donor_term, acceptor_term), 'dp'), 'seq')]
  transfers between devices with their start and end apart: 8 -> 9, of which waited for: 4 -> 5; matrix products, arithmetic and copies ran while one was open for 9% -> 8% of each run, Pallas kernels for 0% -> 0%
where the time goes in v1:
time: 488 us; the launch traced here: 486 us
  waiting for transfers between devices  368 us (75%)
  matrix products  38.8 us (8%)
  starting transfers between devices  31.8 us (7%)
  other arithmetic  19.1 us (4%)
  between operations  14.4 us (3%)
  local copies, waits for them, and re-layouts  14.3 us (3%)
    psum x1, waiting for transfers between devices, on_device(): lax.psum(lax.psum((donor_term, acceptor_term), 'dp'), 'seq')  198 us
    psum x1, waiting for transfers between devices, on_device(): lax.psum((donor_term, acceptor_term), 'dp')  151 us
    dot_general x5, matrix products, on_device(): jnp.dot(upsampled[shift_index:shift_index + row_count], conv_weight[shift...  20.8 us
    all_to_all x1, starting transfers between devices, on_device(): lax.all_to_all(requests, 'seq', split_axis=0, concat_axis=0, tiled=True)  11.7 us
  transfers between devices with their start and end apart: 9, of which 5 were waited for; matrix products, arithmetic and copies ran while one was open for 8% of the time, Pallas kernels for 0%

profile of v1, /device:TPU:2, one launch (start us, length us, event | category | flops | bytes accessed | tf_op | source)
XLA Modules:
  0.0 486.3 jit_solution(9486862294446885583)
XLA Ops:
  7.2 0.8 fusion.89
  8.0 3.5 collective-permute-start
  11.5 1.3 collective-permute-start.1
  12.8 0.7 and_select_fusion
  13.5 0.1 fusion.71
  13.6 0.1 reduce_window_sum.11
  13.7 0.2 select_reduce_fusion
  13.8 0.7 fusion.77
  14.5 0.8 scatter_custom_fusion
  15.3 0.7 all_to_all.12
  16.0 11.7 %all-to-all-start = ((s32[16,1,8]{2,1,0:T(1,128)}), s32[16,1,8]{2,1,0:T(1,128)S(1)}, u32[]{:S(2)}, u32[]{:S(2)}) async-start(s32[16,1,8]{2,1,0:T(1,128)} %bitcast.16), calls=%async_computation | async-start | bytes 16384 | tf_op jit(solution)/shard_map/all_to_all | solution.py:79
  27.7 1.6 broadcast_in_dim.14
  29.3 0.4 slice.107
  29.8 3.6 fusion.20
  33.4 2.8 all-to-all-done
  36.2 0.5 broadcast.232
  36.7 0.7 reduce.3
  37.4 0.1 reshape.228
  37.5 0.1 maximum_bitcast_fusion
  37.6 0.5 broadcast_in_dim.13
  38.2 1.4 reshape.227
  39.6 4.0 fusion.16
  43.6 3.6 fusion.24
  47.1 1.0 fusion.59
  48.1 0.5 broadcast_in_dim.15
  48.7 0.4 slice.113
  49.1 3.6 fusion.12
  52.7 0.5 broadcast_in_dim.12
  53.3 0.4 slice.101
  53.7 6.1 %multiply_convert_fusion = (bf16[512,768]{1,0:T(8,128)(2,1)S(1)}, f32[512,768]{1,0:T(8,128)}) fusion(f32[512,768]{1,0:T(8,128)} %fusion.12, f32[512,768]{1,0:T(8,128)} %fusion.16, f32[512,768]{1,0:T(8,128)} %fusion.20, f32[512,768]{1,0:T(8,128)} %fusion.24, bf16[512,1024]{1,0:T(8,128)(2,1)S(1)} %slice.101, bf16[5,1024,768]{2,1,0:T(8,128)(2,1)} %param.12, ...), kind=kOutput, calls=%fused_computation.41 | convolution fusion | flops 811204608 | bytes 12058624 | tf_op jit(solution)/shard_map/dot_general | solution.py:53
  59.8 0.9 gather_fusion.1
  60.7 1.0 fusion.40
  61.7 5.3 %all-to-all-start.1 = ((bf16[16,8,768]{2,1,0:T(8,128)(2,1)}), bf16[16,8,768]{2,1,0:T(8,128)(2,1)S(1)}, u32[]{:S(2)}, u32[]{:S(2)}) async-start(bf16[16,8,768]{2,1,0:T(8,128)(2,1)} %fusion.40), calls=%async_computation.1 | async-start | bytes 393216 | tf_op jit(solution)/shard_map/all_to_all | solution.py:85
  67.1 0.7 fusion.76
  67.8 1.3 gather_fusion
  69.1 8.3 %all-to-all-done.1 = bf16[16,8,768]{2,1,0:T(8,128)(2,1)S(1)} async-done(((bf16[16,8,768]{2,1,0:T(8,128)(2,1)}), bf16[16,8,768]{2,1,0:T(8,128)(2,1)S(1)}, u32[]{:S(2)}, u32[]{:S(2)}) %all-to-all-start.1) | async-done | bytes 196640 | tf_op jit(solution)/shard_map/all_to_all | solution.py:85
  77.4 0.7 gather_fusion.2
  78.1 1.3 fusion.60
  79.5 0.5 multiply_bitcast_fusion
  80.0 1.7 scatter_custom_fusion.2
  81.7 3.5 all-to-all-start.2
  85.2 0.2 all-reduce.7.cloned.1.call-start
  85.5 2.0 fusion.72
  87.4 7.9 %all-to-all-done.2 = bf16[16,8,768]{2,1,0:T(8,128)(2,1)S(1)} async-done(((bf16[16,8,768]{2,1,0:T(8,128)(2,1)}), bf16[16,8,768]{2,1,0:T(8,128)(2,1)S(1)}, u32[]{:S(2)}, u32[]{:S(2)}) %all-to-all-start.2) | async-done | bytes 196640 | tf_op jit(solution)/shard_map/all_to_all | solution.py:107
  95.3 2.0 fusion.63
  97.3 0.0 all-reduce.5.cloned.1.call-start
  97.3 150.8 %all-reduce.7.cloned.1.call-done = (f32[768,768]{1,0:T(8,128)}, f32[768,768]{1,0:T(8,128)}) async-done(((f32[768,768]{1,0:T(8,128)}, f32[768,768]{1,0:T(8,128)}), (f32[768,768]{1,0:T(8,128)}, f32[768,768]{1,0:T(8,128)})) %all-reduce.7.cloned.1.call-update) | async-done | bytes 4718608 | tf_op jit(solution)/shard_map/psum | solution.py:137
  248.2 1.2 bitcast_convert_fusion
  249.5 1.8 fusion.74
  251.2 1.6 scatter_fusion
  252.8 0.5 fusion.65
  253.4 2.0 scatter_fusion.1
  255.4 2.6 fusion.6
  258.0 1.6 collective-permute-start.2
  259.6 2.4 fusion.18
  262.0 4.5 collective-permute-start.3
  266.6 2.6 fusion.26
  269.2 1.0 fusion.22
  270.3 1.0 fusion.14
  271.3 2.4 add_add_fusion
  273.7 2.5 reshape.233
  276.2 3.6 reduce_sum.35
  279.8 198.0 %all-reduce.5.cloned.1.call-done = (f32[768,768]{1,0:T(8,128)}, f32[768,768]{1,0:T(8,128)}) async-done(((f32[768,768]{1,0:T(8,128)}, f32[768,768]{1,0:T(8,128)}), (f32[768,768]{1,0:T(8,128)}, f32[768,768]{1,0:T(8,128)})) %all-reduce.5.cloned.1.call-update) | async-done | bytes 4718608 | tf_op jit(solution)/shard_map/psum | solution.py:137
  477.7 1.7 dynamic-slice_multiply_fusion
  (34 shorter events, 0.1 us)
Async XLA Ops:
  7.2 53.5 %copy-start = (bf16[768,768]{1,0:T(8,128)(2,1)S(1)}, bf16[768,768]{1,0:T(8,128)(2,1)}, u32[]{:S(2)}) copy-start(bf16[768,768]{1,0:T(8,128)(2,1)} %param.14) | copy-start | bytes 3538948
  8.0 29.4 %collective-permute-start = (bf16[1,1,1024]{2,1,0:T(2,128)(2,1)S(1)}, bf16[1,1,1024]{2,1,0:T(2,128)(2,1)S(1)}, u32[]{:S(2)}, u32[]{:S(2)}) collective-permute-start(bf16[1,1,1024]{2,1,0:T(2,128)(2,1)S(1)} %get-tuple-element.12), channel_id=1, source_target_pairs={{0,1},{1,2},{2,3},{3,4},{4,5},{5,6},{6,7},{7,8},{8,9},{9,10},{10,1... | collective-permute-start | bytes 6152 | tf_op jit(solution)/shard_map/ppermute | solution.py:18
  11.5 26.0 %collective-permute-start.1 = (bf16[1,1,1024]{2,1,0:T(2,128)(2,1)S(1)}, bf16[1,1,1024]{2,1,0:T(2,128)(2,1)S(1)}, u32[]{:S(2)}, u32[]{:S(2)}) collective-permute-start(bf16[1,1,1024]{2,1,0:T(2,128)(2,1)S(1)} %get-tuple-element.13), channel_id=1, source_target_pairs={{1,0},{2,1},{3,2},{4,3},{5,4},{6,5},{7,6},{8,7},{9,8},{10,9},{11,1... | collective-permute-start | bytes 6152 | tf_op jit(solution)/shard_map/ppermute | solution.py:20
  14.5 52.6 %copy-start.8 = (s32[64]{0:T(128)}, s32[64]{0:T(128)S(1)}, u32[]{:S(2)}) copy-start(s32[64]{0:T(128)S(1)} %fusion.77) | copy-start | bytes 772
  16.0 20.2 %all-to-all-start = ((s32[16,1,8]{2,1,0:T(1,128)}), s32[16,1,8]{2,1,0:T(1,128)S(1)}, u32[]{:S(2)}, u32[]{:S(2)}) async-start(s32[16,1,8]{2,1,0:T(1,128)} %bitcast.16), calls=%async_computation | async-start | bytes 16384 | tf_op jit(solution)/shard_map/all_to_all | solution.py:79
  29.8 7.7 %copy-start.1 = (bf16[1,256,1024]{2,1,0:T(8,128)(2,1)S(1)}, bf16[1,256,1024]{2,1,0:T(8,128)(2,1)}, u32[]{:S(2)}) copy-start(bf16[1,256,1024]{2,1,0:T(8,128)(2,1)} %param.10) | copy-start | bytes 1572868
  39.6 4.0 copy-start.4
  49.1 3.6 copy-start.3
  60.7 17.4 %copy-start.2 = (bf16[768,768]{1,0:T(8,128)(2,1)S(1)}, bf16[768,768]{1,0:T(8,128)(2,1)}, u32[]{:S(2)}) copy-start(bf16[768,768]{1,0:T(8,128)(2,1)} %param.13) | copy-start | bytes 3538948
  61.7 15.7 %all-to-all-start.1 = ((bf16[16,8,768]{2,1,0:T(8,128)(2,1)}), bf16[16,8,768]{2,1,0:T(8,128)(2,1)S(1)}, u32[]{:S(2)}, u32[]{:S(2)}) async-start(bf16[16,8,768]{2,1,0:T(8,128)(2,1)} %fusion.40), calls=%async_computation.1 | async-start | bytes 393216 | tf_op jit(solution)/shard_map/all_to_all | solution.py:85
  69.1 10.3 %copy-start.6 = (f32[1,64]{1,0:T(1,128)S(1)}, f32[1,64]{1,0:T(1,128)}, u32[]{:S(2)}) copy-start(f32[1,64]{1,0:T(1,128)} %param.16) | copy-start | bytes 772
  69.1 10.3 %copy-start.7 = (s32[1,64]{1,0:T(1,128)S(1)}, s32[1,64]{1,0:T(1,128)}, u32[]{:S(2)}) copy-start(s32[1,64]{1,0:T(1,128)} %param.19) | copy-start | bytes 772
  77.4 8.1 %copy-start.5 = (bf16[64,768]{1,0:T(8,128)(2,1)S(1)}, bf16[64,768]{1,0:T(8,128)(2,1)}, u32[]{:S(2)}) copy-start(bf16[64,768]{1,0:T(8,128)(2,1)} %gather_fusion) | copy-start | bytes 294916
  81.7 13.6 %all-to-all-start.2 = ((bf16[16,8,768]{2,1,0:T(8,128)(2,1)}), bf16[16,8,768]{2,1,0:T(8,128)(2,1)S(1)}, u32[]{:S(2)}, u32[]{:S(2)}) async-start(bf16[16,8,768]{2,1,0:T(8,128)(2,1)} %bitcast.23), calls=%async_computation.2 | async-start | bytes 393216 | tf_op jit(solution)/shard_map/all_to_all | solution.py:107
  85.2 163.0 %all-reduce.7.cloned.1.call-start = ((), (), s32[]{:S(2)}) async-start(), calls=%async_computation.4 | async-start | bytes 9437184 | tf_op jit(solution)/shard_map/psum | solution.py:137
  97.3 380.4 %all-reduce.5.cloned.1.call-start = ((), (), s32[]{:S(2)}) async-start(), calls=%async_computation.3 | async-start | bytes 9437184 | tf_op jit(solution)/shard_map/psum | solution.py:137
  255.4 13.8 %slice-start = ((s8[7864320]{0:T(1024)(128)(4,1)}), s8[4194304]{0:T(1024)(128)(4,1)S(1)}, s32[]{:S(2)}) async-start(s8[7864320]{0:T(1024)(128)(4,1)} %bitcast.130), calls=%async_computation.5 | async-start | bytes 8388608
  258.0 11.2 %slice-start.1 = ((s8[7864320]{0:T(1024)(128)(4,1)}), s8[3670016]{0:T(1024)(128)(4,1)S(1)}, s32[]{:S(2)}) async-start(s8[7864320]{0:T(1024)(128)(4,1)} %bitcast.130), calls=%async_computation.6 | async-start | bytes 7340032
  258.0 8.5 %collective-permute-start.2 = (bf16[1,2,768]{2,1,0:T(2,128)(2,1)S(1)}, bf16[1,2,768]{2,1,0:T(2,128)(2,1)S(1)}, u32[]{:S(2)}, u32[]{:S(2)}) collective-permute-start(bf16[1,2,768]{2,1,0:T(2,128)(2,1)S(1)} %get-tuple-element.8), channel_id=1, source_target_pairs={{1,0},{2,1},{3,2},{4,3},{5,4},{6,5},{7,6},{8,7},{9,8},{10,9},{11,1... | collective-permute-start | bytes 9224 | tf_op jit(solution)/shard_map/ppermute | solution.py:20
  262.0 8.2 %collective-permute-start.3 = (bf16[1,2,768]{2,1,0:T(2,128)(2,1)S(1)}, bf16[1,2,768]{2,1,0:T(2,128)(2,1)S(1)}, u32[]{:S(2)}, u32[]{:S(2)}) collective-permute-start(bf16[1,2,768]{2,1,0:T(2,128)(2,1)S(1)} %get-tuple-element.9), channel_id=1, source_target_pairs={{0,1},{1,2},{2,3},{3,4},{4,5},{5,6},{6,7},{7,8},{8,9},{9,10},{10,1... | collective-permute-start | bytes 9224 | tf_op jit(solution)/shard_map/ppermute | solution.py:18
Sparse Core Ops, SparseCore 0:
  97.4 150.7 all-reduce.6
  250.9 226.7 all-reduce.4
